TPU v7x, 32 devices: a whole 2x2x4 slice. The times are simulated.
32 devices in a mesh: groups: 2 (over y), dp: 4 (over z), tensor: 4 (over x, core).
Axes of the slice: x: 2, y: 2, z: 4, core: 2. Of those that a mesh axis runs over, the one named last changes fastest.
Arguments:
- kv_cache: bfloat16 [256, 128, 2048], P(('groups', 'dp'), None, 'tensor'), parts along dimension 0
- lengths: int32 [256], P(('groups', 'dp')), parts along dimension 0, may hold values from 1 to 128, as said below
- source: int32 [256], P(('groups', 'dp')), parts along dimension 0, may hold values from 0 to 127, as said below
- queries: bfloat16 [256, 16, 2048], P(('groups', 'dp'), None, 'tensor'), parts along dimension 0, may hold values from -6 to 6
- fresh_kv: bfloat16 [256, 16, 2048], P(('groups', 'dp'), None, 'tensor'), parts along dimension 0, may hold values from -6 to 6
- out_weight: bfloat16 [2048, 4608], P('tensor')
- norm_gain: float32 [4608], P('tensor'), may hold values from 0.5 to 1.5
Outputs:
- normed: bfloat16 [256, 16, 4608], P(('groups', 'dp'), None, 'tensor'), parts along dimension 0
There are 2 independent parts, one for each index of `groups`. A program takes and returns all parts, laid end to end along the dimension named above; an argument that names none is the same for every part. Nothing has to cross between parts.
Inputs may be any that keep to these rules, and one draw needn't show every extreme that they name: `source`: A permutation of the slots. A session may stay on its device or move to another; at most 8 sessions go from one device to any one device, and some device sends 8 to one device. Every device receives 32 sessions, one from each old slot number. `lengths`: some session has 128 cached tokens.
All inputs are finite; a program needn't handle non-finite values.
Results may differ from a plain program's by a relative error of at most 0.018.
Values may be sent and summed in bfloat16 or wider, within the bound.
A program may use at most 64 MiB of HBM per device.

v0:
```python
import jax
import jax.numpy as jnp
from jax import lax
from jax.sharding import PartitionSpec as P

HEAD = 128
QHEADS = 16
KVHEADS = 8


score_scale = 144.0 ** (-0.5)
soft_cap = 50.0
norm_eps = 1e-06


def attend(queries, cached, lengths, fresh_kv):
    slot_count, row_count, query_width = queries.shape
    cache_length = cached.shape[1]
    group_size = QHEADS // KVHEADS
    kv_heads = cached.shape[2] // (2 * HEAD)
    key_values = jnp.concatenate([cached, fresh_kv], axis=1)
    key_values = key_values.reshape(slot_count, cache_length + row_count, kv_heads, 2, HEAD)
    key_rows = key_values[:, :, :, 0]
    value_rows = key_values[:, :, :, 1]
    grouped = queries.reshape(slot_count, row_count, kv_heads, group_size, HEAD)
    scores = (
        jnp.einsum("srkgh,sjkh->skgrj", grouped, key_rows, preferred_element_type=jnp.float32)
        * score_scale
    )
    capped = soft_cap * jnp.tanh(scores / soft_cap)
    position = jnp.arange(cache_length + row_count, dtype=jnp.int32)
    row_position = jnp.arange(row_count, dtype=jnp.int32)
    in_cache = position[None, None, :] < lengths[:, None, None]
    in_block = (position[None, :] >= cache_length) & (
        position[None, :] - cache_length <= row_position[:, None]
    )
    visible = in_cache | in_block[None]
    weights = jnp.where(visible[:, None, None], jnp.exp(capped), 0.0)
    soft_weights = (weights / jnp.sum(weights, axis=-1, keepdims=True)).astype(jnp.bfloat16)
    attended = jnp.einsum(
        "skgrj,sjkh->srkgh", soft_weights, value_rows, preferred_element_type=jnp.float32
    )
    return attended.reshape(slot_count, row_count, query_width).astype(jnp.bfloat16)


def lane_plan(all_source, slot_count, dp_count):
    sessions = all_source.shape[0]
    session_ids = jnp.arange(sessions, dtype=jnp.int32)
    matches = all_source[None, :] == session_ids[:, None]
    new_slot = jnp.sum(jnp.where(matches, session_ids[None, :], 0), axis=1)
    new_home = (new_slot // slot_count).reshape(dp_count, slot_count)
    slot_ids = jnp.arange(slot_count, dtype=jnp.int32)
    earlier = slot_ids[None, :] < slot_ids[:, None]
    same_home = new_home[:, :, None] == new_home[:, None, :]
    lane_ranks = jnp.sum(same_home & earlier[None], axis=2)
    return (new_home, lane_ranks)


def pack_lanes(payload, slot_lanes, lane_count):
    lane_ids = jnp.arange(lane_count, dtype=jnp.int32)
    slot_ids = jnp.arange(payload.shape[0], dtype=jnp.int32)
    lane_hits = slot_lanes[None, :] == lane_ids[:, None]
    filled = jnp.any(lane_hits, axis=1)
    chosen = jnp.sum(jnp.where(lane_hits, slot_ids[None, :], 0), axis=1)
    picked = jnp.take(payload, chosen, axis=0)
    return jnp.where(filled[:, None, None], picked, jnp.zeros((), payload.dtype))


def shards(kv_cache, lengths, source, queries, fresh_kv, out_weight, norm_gain):
    dp_count = lax.axis_size("dp")
    my_index = lax.axis_index("dp")
    slot_count = kv_cache.shape[0]
    pair_cap = max(1, slot_count // dp_count)
    lane_count = dp_count * pair_cap
    old_home = source // slot_count
    all_source, all_lengths = (
        lax.all_gather(source, "dp", axis=0, tiled=True),
        lax.all_gather(lengths, "dp", axis=0, tiled=True),
    )
    new_home, lane_ranks = lane_plan(all_source, slot_count, dp_count)
    out_lanes = new_home[my_index] * pair_cap + lane_ranks[my_index]
    in_lanes = old_home * pair_cap + lane_ranks.reshape(-1)[source]
    sending = pack_lanes(kv_cache, out_lanes, lane_count)
    arrived = lax.all_to_all(sending, "dp", split_axis=0, concat_axis=0, tiled=True)
    moved_rows = jnp.take(arrived, in_lanes, axis=0)
    attended = attend(queries, moved_rows, all_lengths[source], fresh_kv)
    row_total = slot_count * queries.shape[1]
    flat_rows = attended.reshape(row_total, attended.shape[2])
    partial_value = jnp.dot(flat_rows, out_weight, preferred_element_type=jnp.float32)
    tensor_count = lax.axis_size("tensor")
    model_width = out_weight.shape[1]
    own_cols = model_width // tensor_count
    branch = lax.psum(partial_value.astype(jnp.bfloat16), "tensor").astype(jnp.float32)
    mean_square = jnp.mean(branch * branch, axis=-1, keepdims=True)
    own_part = lax.dynamic_slice_in_dim(branch, lax.axis_index("tensor") * own_cols, own_cols, 1)
    normed = own_part * lax.rsqrt(mean_square + norm_eps) * norm_gain
    return normed.astype(jnp.bfloat16).reshape(slot_count, queries.shape[1], own_cols)


def solution(mesh):
    placed = (
        P(("groups", "dp"), None, "tensor"),
        P(("groups", "dp")),
        P(("groups", "dp")),
        P(("groups", "dp"), None, "tensor"),
        P(("groups", "dp"), None, "tensor"),
        P("tensor", None),
        P("tensor"),
    )
    return jax.shard_map(
        shards,
        mesh=mesh,
        in_specs=placed,
        out_specs=P(("groups", "dp"), None, "tensor"),
        check_vma=False,
    )
```

profile of v0, /device:TPU:27, one launch (start us, length us, event | category | flops | bytes accessed | tf_op | source)
XLA Modules:
  0.0 274.4 jit_solution(564269665837484804)
XLA Ops:
  6.5 1.2 dynamic-slice
  8.4 0.9 dynamic-update-slice
  9.3 0.8 dynamic-update-slice.1
  10.1 4.2 %all-reduce.2 = (s32[128]{0:T(128)S(1)}, s32[128]{0:T(128)S(1)}) all-reduce(s32[128]{0:T(128)S(1)} %dynamic-update-slice, s32[128]{0:T(128)S(1)} %dynamic-update-slice.1), channel_id=1, replica_groups=mesh['groups'=2,'dp'=4,'tensor'=4] {'dp'}, use_global_device_ids=true, to_apply=%add | all-reduce | flops 256 | bytes 2048
  14.3 0.1 select_reduce_fusion
  14.4 0.1 reduce_sum.48
  14.5 0.2 convert_reduce_fusion
  14.8 0.1 select_reduce_fusion.1
  14.9 0.1 fusion.7
  15.0 5.0 %gather_fusion.2 = bf16[32,128,512]{2,1,0:T(8,128)(2,1)} fusion(bf16[32,128,512]{2,1,0:T(8,128)(2,1)} %param.9, s32[1024]{0:T(1024)S(1)} %pad_clamp_fusion.1), kind=kCustom, calls=%fused_computation.clone | custom fusion | bytes 8388736 | tf_op jit(solution)/shard_map/jit(_take)/gather | solution.py:65
  20.0 4.7 %select_select_fusion = bf16[32,128,512]{2,1,0:T(8,128)(2,1)} fusion(bf16[32,128,512]{2,1,0:T(8,128)(2,1)} %gather_fusion.2, pred[32]{0:T(512)(128)(4,1)S(1)} %compare_and_fusion.1, pred[32]{0:T(512)(128)(4,1)S(1)} %fusion.7), kind=kLoop, calls=%fused_computation.7 | loop fusion | flops 4194304 | bytes 8388672 | tf_op jit(solution)/shard_map/jit(_where)/select_n | solution.py:66
  24.7 0.0 copy-start.4
  24.7 0.0 copy-start.2
  24.7 7.1 %all-to-all-start = ((bf16[32,128,512]{2,1,0:T(8,128)(2,1)}), bf16[32,128,512]{2,1,0:T(8,128)(2,1)}, u32[]{:S(2)}, u32[]{:S(2)}) async-start(bf16[32,128,512]{2,1,0:T(8,128)(2,1)} %select_select_fusion), calls=%async_computation | async-start | bytes 8388608 | tf_op jit(solution)/shard_map/all_to_all | solution.py:84
  31.8 0.0 all-reduce.5.cloned.1.call-start
  31.8 0.1 reshape.170
  31.9 0.0 copy-done.4
  31.9 0.7 gather_fusion
  32.6 0.7 gather_fusion.1
  33.3 0.0 copy-done.2
  33.4 0.1 reshape.172
  33.6 0.1 iota_compare_fusion.1
  33.6 0.1 broadcast_or_fusion
  33.7 86.6 %all-to-all-done = bf16[32,128,512]{2,1,0:T(8,128)(2,1)} async-done(((bf16[32,128,512]{2,1,0:T(8,128)(2,1)}), bf16[32,128,512]{2,1,0:T(8,128)(2,1)}, u32[]{:S(2)}, u32[]{:S(2)}) %all-to-all-start) | async-done | bytes 4194336 | tf_op jit(solution)/shard_map/all_to_all | solution.py:84
  120.3 5.0 %gather_fusion.3 = bf16[32,128,512]{2,1,0:T(8,128)(2,1)} fusion(bf16[32,128,512]{2,1,0:T(8,128)(2,1)} %all-to-all-done, s32[1024]{0:T(1024)S(1)} %pad_clamp_fusion), kind=kCustom, calls=%fused_computation.1.clone | custom fusion | bytes 8388736 | tf_op jit(solution)/shard_map/jit(_take)/gather | solution.py:85
  125.3 0.0 copy-start.1
  125.3 2.7 broadcast_select_fusion
  128.0 0.0 copy-done.1
  128.0 2.6 pad_maximum_fusion
  130.6 7.7 %reshape.171 = bf16[32,144,2,2,128]{4,3,2,1,0:T(2,128)(2,1)} reshape(bf16[32,144,512]{2,1,0:T(8,128)(2,1)} %pad_maximum_fusion) | data formatting | bytes 9437184 | tf_op jit(solution)/shard_map/reshape | solution.py:22
  138.3 13.0 %fusion.15 = (bf16[32,144,2,1,128]{4,3,2,1,0:T(2,128)(2,1)S(1)}, bf16[32,144,2,1,128]{4,3,2,1,0:T(2,128)(2,1)}) fusion(bf16[32,144,2,2,128]{4,3,2,1,0:T(2,128)(2,1)} %reshape.171), kind=kLoop, calls=%fused_computation.59 | loop fusion | bytes 9437184 | tf_op jit(solution)/shard_map/slice | solution.py:23
  151.4 1.7 bitcast_select_fusion
  153.1 3.3 %fusion.3 = bf16[32,16,2,2,128]{4,1,3,2,0:T(8,128)(2,1)S(1)} fusion(bf16[32,144,2,1,128]{4,3,2,1,0:T(2,128)(2,1)} %get-tuple-element.11, f32[32,2,2,16,144]{4,3,2,1,0:T(8,128)S(1)} %bitcast_select_fusion), kind=kOutput, calls=%fused_computation.17 | convolution fusion | flops 76351632 | bytes 4063232 | tf_op jit(solution)/shard_map/skgrj,sjkh->srkgh/dot_general | solution.py:40
  156.4 0.5 copy.16
  156.9 0.2 convert_element_type.29
  157.1 6.6 %convolution_convert_fusion = bf16[512,4608]{1,0:T(8,128)(2,1)} fusion(bf16[512,512]{1,0:T(8,128)(2,1)S(1)} %convert_element_type.29, bf16[512,4608]{1,0:T(8,128)(2,1)} %param.14), kind=kOutput, calls=%fused_computation.5 | convolution fusion | flops 2418278400 | bytes 9961472 | tf_op jit(solution)/shard_map/dot_general | solution.py:89
  163.7 0.0 all-reduce.5.cloned.1.call-update
  163.7 97.5 %all-reduce.5.cloned.1.call-done = bf16[512,4608]{1,0:T(8,128)(2,1)} async-done(((bf16[512,4608]{1,0:T(8,128)(2,1)}), bf16[512,4608]{1,0:T(8,128)(2,1)}) %all-reduce.5.cloned.1.call-update) | async-done | bytes 4718608 | tf_op jit(solution)/shard_map/psum | solution.py:93
  261.2 0.0 copy-start
  261.2 3.5 %multiply_reduce_fusion = f32[512]{0:T(512)S(1)} fusion(bf16[512,4608]{1,0:T(8,128)(2,1)} %all-reduce.5.cloned.1.call-done), kind=kLoop, calls=%fused_computation.4 | loop fusion | flops 7077376 | bytes 4720640 | tf_op jit(solution)/shard_map/reduce_sum | solution.py:94
  264.7 0.3 copy-done
  265.0 0.0 copy-start.3
  265.0 1.2 convert_element_type.31
  266.2 0.0 copy-done.3
  266.2 1.3 multiply_convert_fusion
  (16 shorter events, 0.1 us)
Async XLA Ops:
  24.7 7.2 %copy-start.4 = (s32[32]{0:T(128)S(1)}, s32[32]{0:T(128)}, u32[]{:S(2)}) copy-start(s32[32]{0:T(128)} %param.11) | copy-start | bytes 388
  24.7 8.6 %copy-start.2 = (bf16[32,16,512]{2,1,0:T(8,128)(2,1)S(1)}, bf16[32,16,512]{2,1,0:T(8,128)(2,1)}, u32[]{:S(2)}) copy-start(bf16[32,16,512]{2,1,0:T(8,128)(2,1)} %param.12) | copy-start | bytes 1572868
  24.7 95.6 %all-to-all-start = ((bf16[32,128,512]{2,1,0:T(8,128)(2,1)}), bf16[32,128,512]{2,1,0:T(8,128)(2,1)}, u32[]{:S(2)}, u32[]{:S(2)}) async-start(bf16[32,128,512]{2,1,0:T(8,128)(2,1)} %select_select_fusion), calls=%async_computation | async-start | bytes 8388608 | tf_op jit(solution)/shard_map/all_to_all | solution.py:84
  31.8 229.4 %all-reduce.5.cloned.1.call-start = ((), (), s32[]{:S(2)}) async-start(), calls=%async_computation.1 | async-start | bytes 9437184 | tf_op jit(solution)/shard_map/psum | solution.py:93
  125.3 2.7 copy-start.1
  261.2 3.8 %copy-start = (bf16[512,4608]{1,0:T(8,128)(2,1)S(1)}, bf16[512,4608]{1,0:T(8,128)(2,1)}, u32[]{:S(2)}) copy-start(bf16[512,4608]{1,0:T(8,128)(2,1)} %all-reduce.5.cloned.1.call-done) | copy-start | bytes 14155780
  265.0 1.2 copy-start.3
Sparse Core Ops, SparseCore 0:
  163.9 97.3 all-reduce.4
where the time goes:
time: 277 us; the launch traced here: 274 us
  waiting for transfers between devices  184 us (66%)
  local copies, waits for them, and re-layouts  36.3 us (13%)
  other arithmetic  16.8 us (6%)
  between operations  14.2 us (5%)
  matrix products  11.6 us (4%)
  starting transfers between devices  7.14 us (3%)
  blocking collectives  4.18 us (2%)
    psum x1, waiting for transfers between devices, shards(): lax.psum(partial_value.astype(jnp.bfloat16), 'tensor').astype(jnp.float32)  97.5 us
    all_to_all x1, waiting for transfers between devices, shards(): lax.all_to_all(sending, 'dp', split_axis=0, concat_axis=0, tiled=True)  86.6 us
    slice x1, local copies, waits for them, and re-layouts, attend(): key_rows = key_values[:, :, :, 0]  13 us
    reshape x1, local copies, waits for them, and re-layouts, attend(): key_values.reshape(slot_count, cache_length + row_count, kv_heads, 2, HEAD)  7.7 us
    all_to_all x1, starting transfers between devices, shards(): lax.all_to_all(sending, 'dp', split_axis=0, concat_axis=0, tiled=True)  7.14 us
    dot_general x1, matrix products, shards(): jnp.dot(flat_rows, out_weight, preferred_element_type=jnp.float32)  6.62 us
  transfers between devices with their start and end apart: 2, of which 2 were waited for; matrix products, arithmetic and copies ran while one was open for 1% of the time, Pallas kernels for 0%

commit v1 on v0

v1 whole, which is shorter than its diff:
```python
import functools

import jax
import jax.numpy as jnp
from jax import lax
from jax.experimental import pallas as pl
from jax.experimental.pallas import tpu as pltpu
from jax.sharding import PartitionSpec as P

HEAD = 128
QHEADS = 16
KVHEADS = 8
GROUP = QHEADS // KVHEADS

score_scale = 144.0 ** (-0.5)
soft_cap = 50.0
norm_eps = 1e-06

MESH = pl.DeviceIdType.MESH
NT = (((1,), (1,)), ((), ()))


def capped_exp(scores):
    return jnp.exp(soft_cap * jnp.tanh(scores * (score_scale / soft_cap)))


def kernel(
    dp_count,
    tensor_count,
    cap,
    model_width,
    lengths,
    slot_of_lane,
    lane_of_slot,
    old_slot_of_lane,
    old_slots,
    gain,
    kv_hbm,
    q_hbm,
    fresh_hbm,
    w_hbm,
    out,
    kv,
    q,
    fresh,
    w,
    ql,
    fl,
    q_in,
    idx_in,
    idx_smem,
    res_out,
    res_in,
    den_out,
    den_in,
    fresh_acc,
    att,
    part_out,
    part_in,
    branch,
    ss_out,
    ss_in,
    local_sem,
    w_send,
    w_recv,
    q_send,
    q_recv,
    i_send,
    i_recv,
    s_sem,
    r_send,
    r_recv,
    d_send,
    d_recv,
    a_send,
    a_recv,
    p_send,
    p_recv,
    n_send,
    n_recv,
):
    slots, rows, q_width = q.shape
    cache_len = kv.shape[1]
    kv_heads = kv.shape[2] // (2 * HEAD)
    q_heads = q_width // HEAD
    halves = tensor_count // 2
    own_cols = out.shape[2]
    chunks, chunk_rows, _ = att.shape
    chunk_lanes = slots // chunks
    per_chunk = chunk_lanes // cap
    depth = w_hbm.shape[-2]

    me = lax.axis_index("dp")
    my_t = lax.axis_index("tensor")
    partner = my_t + 1 - 2 * lax.rem(my_t, 2)

    def dp_peer(o):
        return lax.rem(me + o, dp_count)

    def t_peer(u):
        return lax.rem(my_t + u, tensor_count)

    def w_block(block):
        if len(w_hbm.shape) == 3:
            return w_hbm.at[block]
        return w_hbm.at[:, pl.ds(pl.multiple_of(block * own_cols, 128), own_cols)]

    load_q = pltpu.make_async_copy(q_hbm, q, local_sem.at[0])
    load_fresh = pltpu.make_async_copy(fresh_hbm, fresh, local_sem.at[1])
    load_kv = pltpu.make_async_copy(kv_hbm, kv, local_sem.at[2])
    load_w = [
        pltpu.make_async_copy(
            w_block(t_peer(2 * m)), w.at[m, pl.ds(0, depth)], local_sem.at[3 + m]
        )
        for m in range(halves)
    ]
    load_q.start()
    load_fresh.start()
    load_kv.start()
    for m in range(halves):
        load_w[m].start()

    barrier = pltpu.get_barrier_semaphore()
    for o in range(1, dp_count):
        pl.semaphore_signal(barrier, 1, device_id={"dp": dp_peer(o)}, device_id_type=MESH)
    for u in range(1, tensor_count):
        pl.semaphore_signal(barrier, 1, device_id={"tensor": t_peer(u)}, device_id_type=MESH)
    pl.semaphore_wait(barrier, dp_count - 1 + tensor_count - 1)

    def remote(src, dst, send, recv, where):
        return pltpu.make_async_remote_copy(
            src_ref=src, dst_ref=dst, send_sem=send, recv_sem=recv, device_id=where, device_id_type=MESH
        )

    send_w = [
        remote(
            w_block(lax.rem(partner + 2 * m, tensor_count)),
            w.at[m, pl.ds(depth, depth)],
            w_send.at[m],
            w_recv.at[m],
            {"tensor": partner},
        )
        for m in range(halves)
    ]
    send_q, send_i, send_r, send_d = {}, {}, {}, {}
    for o in range(1, dp_count):
        lanes = pl.ds(o * cap, cap)
        there, back = {"dp": dp_peer(o)}, {"dp": dp_peer(dp_count - o)}
        send_q[o] = remote(ql.at[lanes], q_in.at[lanes], q_send.at[o], q_recv.at[o], there)
        send_i[o] = remote(old_slots.at[o], idx_in.at[o], i_send.at[o], i_recv.at[o], there)
        send_r[o] = remote(res_out.at[lanes], res_in.at[lanes], r_send.at[o], r_recv.at[o], back)
        send_d[o] = remote(den_out.at[o], den_in.at[o], d_send.at[o], d_recv.at[o], back)
    send_a = [
        remote(
            att.at[c, :, pl.ds(0, q_width)],
            att.at[c, :, pl.ds(q_width, q_width)],
            a_send.at[c],
            a_recv.at[c],
            {"tensor": partner},
        )
        for c in range(chunks)
    ]
    send_p = {
        (c, m): remote(
            part_out.at[c, m], part_in.at[c, m], p_send.at[c, m], p_recv.at[c, m], {"tensor": t_peer(2 * m)}
        )
        for c in range(chunks)
        for m in range(1, halves)
    }
    send_n = {
        (c, u): remote(ss_out.at[c], ss_in.at[c, u], n_send.at[c, u], n_recv.at[c, u], {"tensor": t_peer(u)})
        for c in range(chunks)
        for u in range(1, tensor_count)
    }

    load_q.wait()

    def to_lane(lane, _):
        ql[lane] = q[slot_of_lane[lane]]
        return 0

    lax.fori_loop(0, slots, to_lane, 0, unroll=8)
    for o in range(1, dp_count):
        send_i[o].start()
        send_q[o].start()
    for m in range(halves - 1, -1, -1):
        send_w[m].start()
    load_fresh.wait()

    def fresh_to_lane(lane, _):
        fl[lane] = fresh[slot_of_lane[lane]]
        return 0

    lax.fori_loop(0, slots, fresh_to_lane, 0, unroll=8)
    load_kv.wait()

    column = lax.broadcasted_iota(jnp.int32, (rows, HEAD), 1)
    position = lax.broadcasted_iota(jnp.int32, (GROUP * rows, cache_len), 1)
    ones = jnp.ones((cache_len, HEAD), jnp.bfloat16)

    def serve(q_ref, o, slot_at, res, dens):
        total = jnp.zeros((rows, HEAD), jnp.float32)
        for k in range(cap):
            lane = o * cap + k
            slot = slot_at(k)
            length = lengths[slot]
            for h in range(kv_heads):
                first = GROUP * h * HEAD
                asked = jnp.concatenate(
                    [q_ref[lane, :, first + g * HEAD : first + (g + 1) * HEAD] for g in range(GROUP)], axis=0
                )
                keys = kv[slot, :, 2 * h * HEAD : (2 * h + 1) * HEAD]
                values = kv[slot, :, (2 * h + 1) * HEAD : (2 * h + 2) * HEAD]
                scores = lax.dot_general(asked, keys, NT, preferred_element_type=jnp.float32)
                weights = jnp.where(position < length, capped_exp(scores), 0.0).astype(jnp.bfloat16)
                summed = jnp.dot(
                    weights, jnp.concatenate([values, ones], axis=1), preferred_element_type=jnp.float32
                )
                for g in range(GROUP):
                    part = summed[g * rows : (g + 1) * rows]
                    res[lane, :, first + g * HEAD : first + (g + 1) * HEAD] = part[:, :HEAD].astype(jnp.bfloat16)
                    total = jnp.where(column == k * q_heads + GROUP * h + g, part[:, HEAD:], total)
        dens[o] = total

    chunk_keys = chunk_lanes * rows
    row_id = lax.rem(lax.broadcasted_iota(jnp.int32, (GROUP * chunk_keys, chunk_keys), 0), chunk_keys)
    key_id = lax.broadcasted_iota(jnp.int32, (GROUP * chunk_keys, chunk_keys), 1)
    in_block = (row_id // rows == key_id // rows) & (key_id <= row_id)
    fresh_ones = jnp.ones((chunk_keys, HEAD), jnp.bfloat16)

    def fresh_part(c):
        lanes = slice(c * chunk_lanes, (c + 1) * chunk_lanes)
        for h in range(kv_heads):
            first = GROUP * h * HEAD
            asked = jnp.concatenate(
                [
                    ql[lanes, :, first + g * HEAD : first + (g + 1) * HEAD].reshape(chunk_keys, HEAD)
                    for g in range(GROUP)
                ],
                axis=0,
            )
            keys = fl[lanes, :, 2 * h * HEAD : (2 * h + 1) * HEAD].reshape(chunk_keys, HEAD)
            values = fl[lanes, :, (2 * h + 1) * HEAD : (2 * h + 2) * HEAD].reshape(chunk_keys, HEAD)
            scores = lax.dot_general(asked, keys, NT, preferred_element_type=jnp.float32)
            weights = jnp.where(in_block, capped_exp(scores), 0.0).astype(jnp.bfloat16)
            fresh_acc[c, h] = jnp.dot(
                weights, jnp.concatenate([values, fresh_ones], axis=1), preferred_element_type=jnp.float32
            )

    def combine(c):
        for o in range(c * per_chunk, (c + 1) * per_chunk):
            if o:
                send_r[o].wait_recv()
                send_d[o].wait_recv()
        for i in range(chunk_lanes):
            lane = c * chunk_lanes + i
            o, k = lane // cap, lane % cap
            for h in range(kv_heads):
                for g in range(GROUP):
                    head = GROUP * h + g
                    at = slice(g * chunk_keys + i * rows, g * chunk_keys + (i + 1) * rows)
                    cols = slice(head * HEAD, (head + 1) * HEAD)
                    place = k * q_heads + head
                    den = fresh_acc[c, h, at, HEAD:] + den_in[o, :, place : place + 1]
                    num = fresh_acc[c, h, at, :HEAD] + res_in[lane, :, cols].astype(jnp.float32)
                    att[c, i * rows : (i + 1) * rows, cols] = (num / den).astype(jnp.bfloat16)
        send_a[c].start()

    def project(c):
        send_a[c].wait_recv()
        if c == 0:
            for m in range(halves):
                load_w[m].wait()
                send_w[m].wait_recv()
        for m in range(1, halves):
            part_out[c, m] = jnp.dot(att[c], w[m], preferred_element_type=jnp.float32).astype(jnp.bfloat16)
            send_p[c, m].start()
        own = jnp.dot(att[c], w[0], preferred_element_type=jnp.float32)
        branch[c * chunk_lanes : (c + 1) * chunk_lanes] = own.reshape(chunk_lanes, rows, own_cols)

    def gather_sum(c):
        here = slice(c * chunk_lanes, (c + 1) * chunk_lanes)
        total = branch[here].reshape(chunk_rows, own_cols)
        for m in range(1, halves):
            send_p[c, m].wait_recv()
            total = total + part_in[c, m].astype(jnp.float32)
        branch[here] = total.reshape(chunk_lanes, rows, own_cols)
        squares = jnp.sum(total * total, axis=1, keepdims=True)
        ss_out[c] = jnp.transpose(jnp.broadcast_to(squares, (chunk_rows, chunk_rows)))[:8]
        for u in range(1, tensor_count):
            send_n[c, u].start()

    serve(ql, 0, lambda k: old_slot_of_lane[k], res_in, den_in)
    fresh_part(0)
    if per_chunk == 1:
        combine(0)
    for c in range(1, chunks):
        fresh_part(c)
    if per_chunk == 1:
        project(0)
    for o in range(1, dp_count):
        send_i[o].wait_recv()
        spill = pltpu.make_async_copy(idx_in.at[o], idx_smem.at[o], s_sem.at[o])
        spill.start()
        spill.wait()
        send_q[o].wait_recv()
        serve(q_in, o, lambda k, o=o: idx_smem[o, 0, k], res_out, den_out)
        send_d[o].start()
        send_r[o].start()
    for c in range(chunks):
        if c or per_chunk > 1:
            combine(c)
            project(c)
        if c:
            gather_sum(c - 1)
    gather_sum(chunks - 1)

    for c in range(chunks):
        squares = ss_out[c]
        for u in range(1, tensor_count):
            send_n[c, u].wait_recv()
            squares = squares + ss_in[c, u]
        wide = jnp.broadcast_to(squares[:1], (chunk_rows, chunk_rows))
        mean_square = jnp.transpose(wide)[:, :1] * (1.0 / model_width)
        here = slice(c * chunk_lanes, (c + 1) * chunk_lanes)
        scale = lax.rsqrt(mean_square + norm_eps)
        normed = branch[here].reshape(chunk_rows, own_cols) * scale * gain[...]
        branch[here] = normed.reshape(chunk_lanes, rows, own_cols)

    def to_slot(slot, _):
        out[slot] = branch[lane_of_slot[slot]].astype(jnp.bfloat16)
        return 0

    lax.fori_loop(0, slots, to_slot, 0, unroll=4)

    for o in range(1, dp_count):
        for sent in (send_q[o], send_i[o], send_r[o], send_d[o]):
            sent.wait_send()
    for sent in [*send_w, *send_a, *send_p.values(), *send_n.values()]:
        sent.wait_send()


def shards(kv_cache, lengths, source, queries, fresh_kv, out_weight, norm_gain):
    dp_count = lax.axis_size("dp")
    tensor_count = lax.axis_size("tensor")
    slots, rows, q_width = queries.shape
    kv_width = kv_cache.shape[2]
    kv_heads = kv_width // (2 * HEAD)
    cap = max(1, slots // dp_count)
    model_width = out_weight.shape[1]
    true_cols = norm_gain.shape[0]
    own_cols = -(-true_cols // 128) * 128
    depth = out_weight.shape[0]
    halves = tensor_count // 2
    chunk_lanes = max(cap, slots // 4)
    chunks = slots // chunk_lanes
    chunk_rows = chunk_lanes * rows

    if own_cols != true_cols:
        spare = own_cols - true_cols
        blocks = out_weight.reshape(depth, tensor_count, true_cols).transpose(1, 0, 2)
        out_weight = jnp.pad(blocks, ((0, 0), (0, 0), (0, spare)))
        norm_gain = jnp.pad(norm_gain, (0, spare))

    home = source // slots
    offset = (home - lax.axis_index("dp").astype(jnp.int32) + dp_count) % dp_count
    ids = jnp.arange(slots, dtype=jnp.int32)
    same = (offset[:, None] == offset[None, :]) & (ids[None, :] < ids[:, None])
    lane_of_slot = offset * cap + jnp.sum(same.astype(jnp.int32), axis=1)
    hits = lane_of_slot[None, :] == ids[:, None]
    slot_of_lane = jnp.sum(jnp.where(hits, ids[None, :], 0), axis=1)
    old_slot = jnp.sum(jnp.where(hits, (source % slots)[None, :], 0), axis=1)
    old_slots = jnp.pad(old_slot.reshape(dp_count, 1, cap), ((0, 0), (0, 7), (0, 128 - cap)))

    vmem = pl.BlockSpec(memory_space=pltpu.VMEM)
    smem = pl.BlockSpec(memory_space=pltpu.SMEM)
    hbm = pl.BlockSpec(memory_space=pl.ANY)
    dma = pltpu.SemaphoreType.DMA
    bf16, f32, i32 = jnp.bfloat16, jnp.float32, jnp.int32
    normed = pl.pallas_call(
        functools.partial(kernel, dp_count, tensor_count, cap, model_width),
        out_shape=jax.ShapeDtypeStruct((slots, rows, own_cols), bf16),
        in_specs=[smem, smem, smem, smem, vmem, vmem, hbm, hbm, hbm, hbm],
        out_specs=vmem,
        scratch_shapes=[
            pltpu.VMEM(kv_cache.shape, bf16),
            pltpu.VMEM(queries.shape, bf16),
            pltpu.VMEM(fresh_kv.shape, bf16),
            pltpu.VMEM((halves, 2 * depth, own_cols), bf16),
            pltpu.VMEM(queries.shape, bf16),
            pltpu.VMEM(fresh_kv.shape, bf16),
            pltpu.VMEM(queries.shape, bf16),
            pltpu.VMEM((dp_count, 8, 128), i32),
            pltpu.SMEM((dp_count, 8, 128), i32),
            pltpu.VMEM(queries.shape, bf16),
            pltpu.VMEM(queries.shape, bf16),
            pltpu.VMEM((dp_count, rows, 128), f32),
            pltpu.VMEM((dp_count, rows, 128), f32),
            pltpu.VMEM((chunks, kv_heads, GROUP * chunk_rows, 2 * HEAD), f32),
            pltpu.VMEM((chunks, chunk_rows, 2 * q_width), bf16),
            pltpu.VMEM((chunks, halves, chunk_rows, own_cols), bf16),
            pltpu.VMEM((chunks, halves, chunk_rows, own_cols), bf16),
            pltpu.VMEM((slots, rows, own_cols), f32),
            pltpu.VMEM((chunks, 8, 128), f32),
            pltpu.VMEM((chunks, tensor_count, 8, 128), f32),
            dma((3 + halves,)),
            dma((halves,)),
            dma((halves,)),
            *[dma((dp_count,)) for _ in range(9)],
            dma((chunks,)),
            dma((chunks,)),
            dma((chunks, halves)),
            dma((chunks, halves)),
            dma((chunks, tensor_count)),
            dma((chunks, tensor_count)),
        ],
        compiler_params=pltpu.CompilerParams(
            collective_id=0, has_side_effects=True, vmem_limit_bytes=48 * 2**20
        ),
        cost_estimate=pl.CostEstimate(
            flops=2 * slots * rows * depth * own_cols * tensor_count,
            bytes_accessed=2 * (kv_cache.size + out_weight.size),
            transcendentals=0,
        ),
    )(
        lengths,
        slot_of_lane,
        lane_of_slot,
        old_slot,
        old_slots,
        norm_gain.reshape(1, own_cols),
        kv_cache,
        queries,
        fresh_kv,
        out_weight,
    )
    return normed[:, :, :true_cols]


def solution(mesh):
    placed = (
        P(("groups", "dp"), None, "tensor"),
        P(("groups", "dp")),
        P(("groups", "dp")),
        P(("groups", "dp"), None, "tensor"),
        P(("groups", "dp"), None, "tensor"),
        P("tensor", None),
        P("tensor"),
    )
    return jax.shard_map(
        shards,
        mesh=mesh,
        in_specs=placed,
        out_specs=P(("groups", "dp"), None, "tensor"),
        check_vma=False,
    )
```

time: 277 us -> 61.1 us (0.22)
  waiting for transfers between devices: 184 us -> 0 us
  Pallas kernels: 0 us -> 55.3 us
  local copies, waits for them, and re-layouts: 36.3 us -> 4.55 us
  other arithmetic: 16.8 us -> 0.98 us
  between operations: 14.2 us -> 0.03 us
  matrix products: 11.6 us -> 0 us
  starting transfers between devices: 7.14 us -> 0 us
  blocking collectives: 4.18 us -> 0 us
    psum x1 -> x0, waiting for transfers between devices: 97.5 us -> none  [shards(): lax.psum(partial_value.astype(jnp.bfloat16), 'tensor').astype(jnp.float32)]
    all_to_all x1 -> x0, waiting for transfers between devices: 86.6 us -> none  [shards(): lax.all_to_all(sending, 'dp', split_axis=0, concat_axis=0, tiled=True)]
    pallas_call x0 -> x1, Pallas kernels: none -> 55.3 us  [shards(): pl.pallas_call(functools.partial(kernel, dp_count, tensor_count, cap, mod...]
    slice x1 -> x0, local copies, waits for them, and re-layouts: 13 us -> none  [attend(): key_rows = key_values[:, :, :, 0]]
    dot_general x3 -> x0, matrix products: 11.6 us -> none  [the longest x1 6.62 us: shards(): jnp.dot(flat_rows, out_weight, preferred_element_type=jnp.float32)]
    gather x4 -> x0, local copies, waits for them, and re-layouts: 11.3 us -> none  [the longest x1 4.97 us: pack_lanes(): picked = jnp.take(payload, chosen, axis=0)]
    all_to_all x1 -> x0, starting transfers between devices: 7.14 us -> none  [shards(): lax.all_to_all(sending, 'dp', split_axis=0, concat_axis=0, tiled=True)]
    reshape x3 -> x2, local copies, waits for them, and re-layouts: 7.91 us -> 0.8 us  [the longest x1 0.71 us: shards(): norm_gain.reshape(1, own_cols)]
  transfers between devices with their start and end apart: 2 -> 0, of which waited for: 2 -> 0; matrix products, arithmetic and copies ran while one was open for 1% -> 0% of each run, Pallas kernels for 0% -> 0%
where the time goes in v1:
time: 61.1 us; the launch traced here: 60.8 us
  Pallas kernels  55.3 us (91%)
  local copies, waits for them, and re-layouts  4.55 us (7%)
  other arithmetic  0.98 us (2%)
    pallas_call x1, Pallas kernels, shards(): pl.pallas_call(functools.partial(kernel, dp_count, tensor_count, cap, mod...  55.3 us
    unnamed x7, local copies, waits for them, and re-layouts  3.75 us

profile of v1, /device:TPU:27, one launch (start us, length us, event | category | flops | bytes accessed | tf_op | source)
XLA Modules:
  0.0 60.8 jit_solution(14835722141686040694)
XLA Ops:
  0.0 0.7 %and_select_fusion.1 = (s32[32]{0:T(128)S(1)}, s32[32]{0:T(128)S(1)}) fusion(s32[32]{0:T(128)} %param.9, s32[]{:T(128)S(6)} %axis_index.15), kind=kLoop, calls=%fused_computation.9 | loop fusion | flops 1024 | bytes 388 | tf_op jit(solution)/shard_map/jit(remainder)/select_n | solution.py:366
  0.7 0.2 convert_reduce_fusion
  0.9 0.1 select_reduce_fusion
  1.0 0.1 reshape.10
  1.1 0.7 %reshape.11.gain = f32[1,1152]{1,0:T(1,128)S(1)} reshape(f32[1152]{0:T(1024)} %param.13) | data formatting | bytes 9216 | tf_op jit(solution)/shard_map/reshape | solution.py:431
  1.8 0.0 copy-start
  1.8 1.0 %copy-done = bf16[32,16,512]{2,1,0:T(8,128)(2,1)S(1)} copy-done((bf16[32,16,512]{2,1,0:T(8,128)(2,1)S(1)}, bf16[32,16,512]{2,1,0:T(8,128)(2,1)}, u32[]{:S(2)}) %copy-start) | copy-done | bytes 524312
  2.8 0.0 copy-start.1
  2.8 1.0 %copy-done.1 = bf16[32,16,512]{2,1,0:T(8,128)(2,1)S(1)} copy-done((bf16[32,16,512]{2,1,0:T(8,128)(2,1)S(1)}, bf16[32,16,512]{2,1,0:T(8,128)(2,1)}, u32[]{:S(2)}) %copy-start.1) | copy-done | bytes 524312
  3.9 0.0 copy-start.2
  3.9 0.7 %copy-done.2 = s32[32]{0:T(128)S(1)} copy-done((s32[32]{0:T(128)S(1)}, s32[32]{0:T(128)}, u32[]{:S(2)}) %copy-start.2) | copy-done | bytes 152
  4.5 55.3 %shard_map.73 = bf16[32,16,1152]{2,1,0:T(8,128)(2,1)S(1)} custom-call(s32[32]{0:T(128)S(1)} %copy-done.2, s32[32]{0:T(128)S(1)} %get-tuple-element.6.slot_of_lane, s32[32]{0:T(128)S(1)} %multiply_add_fusion.lane_of_slot, s32[32]{0:T(128)S(1)} %get-tuple-element.5.old_slot_of_lane, s32[4,8,128]{2,1,0:T(8,128)S(1)} %pad.4.old_slots, ...), custom_call_target="tpu_custom_call" | custom-call | flops 2415919104 | bytes 8912896 | tf_op jit(solution)/shard_map/pallas_call | solution.py:380
  59.8 1.0 %copy.11 = bf16[32,16,1152]{2,1,0:T(8,128)(2,1)} copy(bf16[32,16,1152]{2,1,0:T(8,128)(2,1)S(1)} %shard_map.73) | data formatting | bytes 2359296
  (2 shorter events, 0.0 us)
Async XLA Ops:
  1.8 1.0 %copy-start = (bf16[32,16,512]{2,1,0:T(8,128)(2,1)S(1)}, bf16[32,16,512]{2,1,0:T(8,128)(2,1)}, u32[]{:S(2)}) copy-start(bf16[32,16,512]{2,1,0:T(8,128)(2,1)} %q_hbm.1) | copy-start | bytes 1572868
  2.8 1.0 %copy-start.1 = (bf16[32,16,512]{2,1,0:T(8,128)(2,1)S(1)}, bf16[32,16,512]{2,1,0:T(8,128)(2,1)}, u32[]{:S(2)}) copy-start(bf16[32,16,512]{2,1,0:T(8,128)(2,1)} %fresh_hbm.1) | copy-start | bytes 1572868
  3.9 0.7 %copy-start.2 = (s32[32]{0:T(128)S(1)}, s32[32]{0:T(128)}, u32[]{:S(2)}) copy-start(s32[32]{0:T(128)} %lengths.1) | copy-start | bytes 388

commit v2 on v1

--- a/solution.py
+++ b/solution.py
@@ -29,12 +29,9 @@
     tensor_count,
     cap,
     model_width,
-    lengths,
-    slot_of_lane,
-    lane_of_slot,
-    old_slot_of_lane,
     old_slots,
     gain,
+    lists_hbm,
     kv_hbm,
     q_hbm,
     fresh_hbm,
@@ -49,6 +46,7 @@
     q_in,
     idx_in,
     idx_smem,
+    lists,
     res_out,
     res_in,
     den_out,
@@ -105,6 +103,16 @@
             return w_hbm.at[block]
         return w_hbm.at[:, pl.ds(pl.multiple_of(block * own_cols, 128), own_cols)]
 
+    def length_of(slot):
+        return lists[slot]
+
+    def slot_of(lane):
+        return lists[slots + lane]
+
+    def lane_of(slot):
+        return lists[2 * slots + slot]
+
+    load_lists = pltpu.make_async_copy(lists_hbm, lists, s_sem.at[0])
     load_q = pltpu.make_async_copy(q_hbm, q, local_sem.at[0])
     load_fresh = pltpu.make_async_copy(fresh_hbm, fresh, local_sem.at[1])
     load_kv = pltpu.make_async_copy(kv_hbm, kv, local_sem.at[2])
@@ -114,10 +122,11 @@
         )
         for m in range(halves)
     ]
+    load_lists.start()
     load_q.start()
+    load_kv.start()
     load_fresh.start()
-    load_kv.start()
-    for m in range(halves):
+    for m in range(halves - 1, -1, -1):
         load_w[m].start()
 
     barrier = pltpu.get_barrier_semaphore()
@@ -125,6 +134,14 @@
         pl.semaphore_signal(barrier, 1, device_id={"dp": dp_peer(o)}, device_id_type=MESH)
     for u in range(1, tensor_count):
         pl.semaphore_signal(barrier, 1, device_id={"tensor": t_peer(u)}, device_id_type=MESH)
+    load_lists.wait()
+    load_q.wait()
+
+    def to_lane(lane, _):
+        ql[lane] = q[slot_of(lane)]
+        return 0
+
+    lax.fori_loop(0, slots, to_lane, 0, unroll=8)
     pl.semaphore_wait(barrier, dp_count - 1 + tensor_count - 1)
 
     def remote(src, dst, send, recv, where):
@@ -173,13 +190,6 @@
         for u in range(1, tensor_count)
     }
 
-    load_q.wait()
-
-    def to_lane(lane, _):
-        ql[lane] = q[slot_of_lane[lane]]
-        return 0
-
-    lax.fori_loop(0, slots, to_lane, 0, unroll=8)
     for o in range(1, dp_count):
         send_i[o].start()
         send_q[o].start()
@@ -188,7 +198,7 @@
     load_fresh.wait()
 
     def fresh_to_lane(lane, _):
-        fl[lane] = fresh[slot_of_lane[lane]]
+        fl[lane] = fresh[slot_of(lane)]
         return 0
 
     lax.fori_loop(0, slots, fresh_to_lane, 0, unroll=8)
@@ -203,7 +213,7 @@
         for k in range(cap):
             lane = o * cap + k
             slot = slot_at(k)
-            length = lengths[slot]
+            length = length_of(slot)
             for h in range(kv_heads):
                 first = GROUP * h * HEAD
                 asked = jnp.concatenate(
@@ -290,30 +300,36 @@
         for u in range(1, tensor_count):
             send_n[c, u].start()
 
-    serve(ql, 0, lambda k: old_slot_of_lane[k], res_in, den_in)
-    fresh_part(0)
-    if per_chunk == 1:
-        combine(0)
-    for c in range(1, chunks):
-        fresh_part(c)
-    if per_chunk == 1:
-        project(0)
-    for o in range(1, dp_count):
+    def answer(o):
         send_i[o].wait_recv()
         spill = pltpu.make_async_copy(idx_in.at[o], idx_smem.at[o], s_sem.at[o])
         spill.start()
         spill.wait()
         send_q[o].wait_recv()
-        serve(q_in, o, lambda k, o=o: idx_smem[o, 0, k], res_out, den_out)
+        serve(q_in, o, lambda k: idx_smem[o, 0, k], res_out, den_out)
         send_d[o].start()
         send_r[o].start()
+
+    alone = per_chunk == 1
+    serve(ql, 0, lambda k: lists[3 * slots + k], res_in, den_in)
+    fresh_part(0)
+    if alone:
+        combine(0)
+        fresh_part(1)
+        project(0)
     for c in range(chunks):
-        if c or per_chunk > 1:
-            combine(c)
-            project(c)
-        if c:
-            gather_sum(c - 1)
-    gather_sum(chunks - 1)
+        for o in range(c * per_chunk, (c + 1) * per_chunk):
+            if o:
+                answer(o)
+        if c + 1 < chunks and not (alone and c == 0):
+            fresh_part(c + 1)
+    for c in range(1 if alone else 0, chunks):
+        combine(c)
+        if c == 1:
+            gather_sum(0)
+        project(c)
+    for c in range(1, chunks):
+        gather_sum(c)
 
     for c in range(chunks):
         squares = ss_out[c]
@@ -324,11 +340,11 @@
         mean_square = jnp.transpose(wide)[:, :1] * (1.0 / model_width)
         here = slice(c * chunk_lanes, (c + 1) * chunk_lanes)
         scale = lax.rsqrt(mean_square + norm_eps)
-        normed = branch[here].reshape(chunk_rows, own_cols) * scale * gain[...]
+        normed = branch[here].reshape(chunk_rows, own_cols) * scale * gain[...].reshape(1, own_cols)
         branch[here] = normed.reshape(chunk_lanes, rows, own_cols)
 
     def to_slot(slot, _):
-        out[slot] = branch[lane_of_slot[slot]].astype(jnp.bfloat16)
+        out[slot] = branch[lane_of(slot)].astype(jnp.bfloat16)
         return 0
 
     lax.fori_loop(0, slots, to_slot, 0, unroll=4)
@@ -370,17 +386,17 @@
     hits = lane_of_slot[None, :] == ids[:, None]
     slot_of_lane = jnp.sum(jnp.where(hits, ids[None, :], 0), axis=1)
     old_slot = jnp.sum(jnp.where(hits, (source % slots)[None, :], 0), axis=1)
+    lists = jnp.concatenate([lengths, slot_of_lane, lane_of_slot, old_slot])
     old_slots = jnp.pad(old_slot.reshape(dp_count, 1, cap), ((0, 0), (0, 7), (0, 128 - cap)))
 
     vmem = pl.BlockSpec(memory_space=pltpu.VMEM)
-    smem = pl.BlockSpec(memory_space=pltpu.SMEM)
     hbm = pl.BlockSpec(memory_space=pl.ANY)
     dma = pltpu.SemaphoreType.DMA
     bf16, f32, i32 = jnp.bfloat16, jnp.float32, jnp.int32
     normed = pl.pallas_call(
         functools.partial(kernel, dp_count, tensor_count, cap, model_width),
         out_shape=jax.ShapeDtypeStruct((slots, rows, own_cols), bf16),
-        in_specs=[smem, smem, smem, smem, vmem, vmem, hbm, hbm, hbm, hbm],
+        in_specs=[vmem, vmem, hbm, hbm, hbm, hbm, hbm],
         out_specs=vmem,
         scratch_shapes=[
             pltpu.VMEM(kv_cache.shape, bf16),
@@ -392,6 +408,7 @@
             pltpu.VMEM(queries.shape, bf16),
             pltpu.VMEM((dp_count, 8, 128), i32),
             pltpu.SMEM((dp_count, 8, 128), i32),
+            pltpu.SMEM((4 * slots,), i32),
             pltpu.VMEM(queries.shape, bf16),
             pltpu.VMEM(queries.shape, bf16),
             pltpu.VMEM((dp_count, rows, 128), f32),
@@ -415,7 +432,7 @@
             dma((chunks, tensor_count)),
         ],
         compiler_params=pltpu.CompilerParams(
-            collective_id=0, has_side_effects=True, vmem_limit_bytes=48 * 2**20
+            collective_id=0, has_side_effects=True, vmem_limit_bytes=60 * 2**20
         ),
         cost_estimate=pl.CostEstimate(
             flops=2 * slots * rows * depth * own_cols * tensor_count,
@@ -423,12 +440,9 @@
             transcendentals=0,
         ),
     )(
-        lengths,
-        slot_of_lane,
-        lane_of_slot,
-        old_slot,
         old_slots,
-        norm_gain.reshape(1, own_cols),
+        norm_gain,
+        lists,
         kv_cache,
         queries,
         fresh_kv,

time: 61.1 us -> 62.2 us (1.018)
  local copies, waits for them, and re-layouts: 4.55 us -> 3.07 us
  other arithmetic: 0.98 us -> 2.29 us
  Pallas kernels: 55.3 us -> 56.6 us
    unnamed x7 -> x1, local copies, waits for them, and re-layouts: 3.75 us -> 2.37 us
    concatenate x0 -> x1, other arithmetic: none -> 1.31 us  [shards(): lists = jnp.concatenate([lengths, slot_of_lane, lane_of_slot, old_slot])]
    pallas_call x1, Pallas kernels: 55.3 us -> 56.6 us  [shards(): pl.pallas_call(functools.partial(kernel, dp_count, tensor_count, cap, mod...]
    reshape x1 -> x0, local copies, waits for them, and re-layouts: 0.71 us -> none  [shards(): norm_gain.reshape(1, own_cols)]
where the time goes in v2:
time: 62.2 us; the launch traced here: 62 us
  Pallas kernels  56.6 us (91%)
  local copies, waits for them, and re-layouts  3.07 us (5%)
  other arithmetic  2.29 us (4%)
    pallas_call x1, Pallas kernels, shards(): pl.pallas_call(functools.partial(kernel, dp_count, tensor_count, cap, mod...  56.6 us
    unnamed x1, local copies, waits for them, and re-layouts  2.37 us
    concatenate x1, other arithmetic, shards(): lists = jnp.concatenate([lengths, slot_of_lane, lane_of_slot, old_slot])  1.31 us

profile of v2, /device:TPU:27, one launch (start us, length us, event | category | flops | bytes accessed | tf_op | source)
XLA Modules:
  0.0 62.0 jit_solution(9860067689589708305)
XLA Ops:
  0.0 0.7 %and_select_fusion = (s32[32]{0:T(128)S(1)}, s32[32]{0:T(128)S(1)}) fusion(s32[32]{0:T(128)} %param.9, s32[]{:T(128)S(6)} %axis_index.15), kind=kLoop, calls=%fused_computation.8 | loop fusion | flops 1024 | bytes 388 | tf_op jit(solution)/shard_map/jit(remainder)/select_n | solution.py:388
  0.7 0.2 convert_reduce_fusion
  0.9 0.1 select_reduce_fusion
  1.0 1.3 %pad_add_fusion.lists_hbm = s32[128]{0:T(128)} fusion(s32[32]{0:T(128)S(1)} %get-tuple-element.6, s32[32]{0:T(128)S(1)} %multiply_add_fusion, s32[32]{0:T(128)S(1)} %get-tuple-element.5, s32[32]{0:T(128)} %param.8), kind=kLoop, calls=%fused_computation.15 | loop fusion | flops 384 | bytes 1024 | tf_op jit(solution)/shard_map/concatenate | solution.py:389
  2.3 0.1 reshape.7
  2.4 0.6 pad.4.old_slots
  3.0 56.6 %shard_map.73 = bf16[32,16,1152]{2,1,0:T(8,128)(2,1)} custom-call(s32[4,8,128]{2,1,0:T(8,128)} %pad.4.old_slots, f32[1152]{0:T(1024)} %gain.1, s32[128]{0:T(128)} %pad_add_fusion.lists_hbm, bf16[32,128,512]{2,1,0:T(8,128)(2,1)} %kv_hbm.1, bf16[32,16,512]{2,1,0:T(8,128)(2,1)} %q_hbm.1, bf16[32,16,512]{2,1,0:T(8,128)(2,1)} %fresh_hbm.1, bf16[512,4608]{1,0:T(8,128)(2,1)} %w_hbm.1), custom_call_target="tpu_custom_call" | custom-call | flops 2415919104 | bytes 8912896 | tf_op jit(solution)/shard_map/pallas_call | solution.py:396
  59.6 2.4 %copy.11 = bf16[32,16,1152]{2,1,0:T(8,128)(2,1)} copy(bf16[32,16,1152]{2,1,0:T(8,128)(2,1)} %shard_map.73) | data formatting | bytes 2359296
  (1 shorter events, 0.0 us)

commit v3 on v2

--- a/solution.py
+++ b/solution.py
@@ -278,13 +278,17 @@
 
     def project(c):
         send_a[c].wait_recv()
-        if c == 0:
-            for m in range(halves):
+        for m in range(1, halves):
+            if c == 0:
                 load_w[m].wait()
                 send_w[m].wait_recv()
-        for m in range(1, halves):
             part_out[c, m] = jnp.dot(att[c], w[m], preferred_element_type=jnp.float32).astype(jnp.bfloat16)
             send_p[c, m].start()
+
+    def project_own(c):
+        if c == 0:
+            load_w[0].wait()
+            send_w[0].wait_recv()
         own = jnp.dot(att[c], w[0], preferred_element_type=jnp.float32)
         branch[c * chunk_lanes : (c + 1) * chunk_lanes] = own.reshape(chunk_lanes, rows, own_cols)
 
@@ -315,19 +319,25 @@
     fresh_part(0)
     if alone:
         combine(0)
+        answer(1)
         fresh_part(1)
         project(0)
-    for c in range(chunks):
-        for o in range(c * per_chunk, (c + 1) * per_chunk):
-            if o:
-                answer(o)
-        if c + 1 < chunks and not (alone and c == 0):
-            fresh_part(c + 1)
+        for o in range(2, dp_count):
+            answer(o)
+        project_own(0)
+        for c in range(2, chunks):
+            fresh_part(c)
+    else:
+        for o in range(1, dp_count):
+            answer(o)
+        for c in range(1, chunks):
+            fresh_part(c)
     for c in range(1 if alone else 0, chunks):
         combine(c)
+        project(c)
+        project_own(c)
         if c == 1:
             gather_sum(0)
-        project(c)
     for c in range(1, chunks):
         gather_sum(c)
 
@@ -432,7 +442,7 @@
             dma((chunks, tensor_count)),
         ],
         compiler_params=pltpu.CompilerParams(
-            collective_id=0, has_side_effects=True, vmem_limit_bytes=60 * 2**20
+            collective_id=0, has_side_effects=True, vmem_limit_bytes=48 * 2**20
         ),
         cost_estimate=pl.CostEstimate(
             flops=2 * slots * rows * depth * own_cols * tensor_count,

time: 62.2 us -> 61.2 us (0.984)
  Pallas kernels: 56.6 us -> 55.3 us
  local copies, waits for them, and re-layouts: 3.07 us -> 3.89 us
    unnamed x1 -> x7, local copies, waits for them, and re-layouts: 2.37 us -> 3.8 us
    pallas_call x1, Pallas kernels: 56.6 us -> 55.3 us  [shards(): pl.pallas_call(functools.partial(kernel, dp_count, tensor_count, cap, mod...]
where the time goes in v3:
time: 61.2 us; the launch traced here: 60.9 us
  Pallas kernels  55.3 us (90%)
  local copies, waits for them, and re-layouts  3.89 us (6%)
  other arithmetic  1.72 us (3%)
    pallas_call x1, Pallas kernels, shards(): pl.pallas_call(functools.partial(kernel, dp_count, tensor_count, cap, mod...  55.3 us
    unnamed x7, local copies, waits for them, and re-layouts  3.8 us

profile of v3, /device:TPU:27, one launch (start us, length us, event | category | flops | bytes accessed | tf_op | source)
XLA Modules:
  0.0 60.9 jit_solution(3525796642608183469)
XLA Ops:
  0.0 0.7 %and_select_fusion = (s32[32]{0:T(128)S(1)}, s32[32]{0:T(128)S(1)}) fusion(s32[32]{0:T(128)} %param.9, s32[]{:T(128)S(6)} %axis_index.15), kind=kLoop, calls=%fused_computation.8 | loop fusion | flops 1024 | bytes 388 | tf_op jit(solution)/shard_map/jit(remainder)/select_n | solution.py:398
  0.7 0.2 convert_reduce_fusion
  0.9 0.1 select_reduce_fusion
  1.0 0.7 %pad_add_fusion.lists_hbm = s32[128]{0:T(128)S(1)} fusion(s32[32]{0:T(128)S(1)} %get-tuple-element.6, s32[32]{0:T(128)S(1)} %multiply_add_fusion, s32[32]{0:T(128)S(1)} %get-tuple-element.5, s32[32]{0:T(128)} %param.8), kind=kLoop, calls=%fused_computation.15 | loop fusion | flops 384 | bytes 1024 | tf_op jit(solution)/shard_map/concatenate | solution.py:399
  1.7 0.1 reshape.7
  1.8 0.0 copy-start
  1.8 1.0 %copy-done = bf16[32,16,512]{2,1,0:T(8,128)(2,1)S(1)} copy-done((bf16[32,16,512]{2,1,0:T(8,128)(2,1)S(1)}, bf16[32,16,512]{2,1,0:T(8,128)(2,1)}, u32[]{:S(2)}) %copy-start) | copy-done | bytes 524312
  2.9 0.0 copy-start.1
  2.9 1.0 %copy-done.1 = bf16[32,16,512]{2,1,0:T(8,128)(2,1)S(1)} copy-done((bf16[32,16,512]{2,1,0:T(8,128)(2,1)S(1)}, bf16[32,16,512]{2,1,0:T(8,128)(2,1)}, u32[]{:S(2)}) %copy-start.1) | copy-done | bytes 524312
  3.9 0.0 copy-start.2
  3.9 0.7 %copy-done.2 = f32[1152]{0:T(1024)S(1)} copy-done((f32[1152]{0:T(1024)S(1)}, f32[1152]{0:T(1024)}, u32[]{:S(2)}) %copy-start.2) | copy-done | bytes 4632
  4.6 55.3 %shard_map.73 = bf16[32,16,1152]{2,1,0:T(8,128)(2,1)S(1)} custom-call(s32[4,8,128]{2,1,0:T(8,128)S(1)} %pad.4.old_slots, f32[1152]{0:T(1024)S(1)} %copy-done.2, s32[128]{0:T(128)S(1)} %pad_add_fusion.lists_hbm, bf16[32,128,512]{2,1,0:T(8,128)(2,1)} %kv_hbm.1, bf16[32,16,512]{2,1,0:T(8,128)(2,1)S(1)} %copy-done, bf16[32,16,512]{2,1,0:T(8,128)(2,1)S(1)} %copy-done.1, ...), custom_call_target="tpu_custom_call" | custom-call | flops 2415919104 | bytes 8912896 | tf_op jit(solution)/shard_map/pallas_call | solution.py:406
  59.9 1.0 %copy.11 = bf16[32,16,1152]{2,1,0:T(8,128)(2,1)} copy(bf16[32,16,1152]{2,1,0:T(8,128)(2,1)S(1)} %shard_map.73) | data formatting | bytes 2359296
  (2 shorter events, 0.0 us)
Async XLA Ops:
  1.8 1.0 %copy-start = (bf16[32,16,512]{2,1,0:T(8,128)(2,1)S(1)}, bf16[32,16,512]{2,1,0:T(8,128)(2,1)}, u32[]{:S(2)}) copy-start(bf16[32,16,512]{2,1,0:T(8,128)(2,1)} %q_hbm.1) | copy-start | bytes 1572868
  2.9 1.0 %copy-start.1 = (bf16[32,16,512]{2,1,0:T(8,128)(2,1)S(1)}, bf16[32,16,512]{2,1,0:T(8,128)(2,1)}, u32[]{:S(2)}) copy-start(bf16[32,16,512]{2,1,0:T(8,128)(2,1)} %fresh_hbm.1) | copy-start | bytes 1572868
  3.9 0.7 %copy-start.2 = (f32[1152]{0:T(1024)S(1)}, f32[1152]{0:T(1024)}, u32[]{:S(2)}) copy-start(f32[1152]{0:T(1024)} %gain.1) | copy-start | bytes 13828
